TPU v7x, 32 devices: a whole 2x2x4 slice. The times are simulated.
32 devices in a mesh: grp: 2 (over x), seq: 16 (over z, y, core).
Axes of the slice: x: 2, y: 2, z: 4, core: 2. Of those that a mesh axis runs over, the one named last changes fastest.
Arguments:
- queries: bfloat16 [128, 5120], P(('grp', 'seq')), parts along dimension 0
- keys: bfloat16 [16384, 5120], P(('grp', 'seq')), parts along dimension 0
- values: bfloat16 [16384, 5120], P(('grp', 'seq')), parts along dimension 0, may hold values from -6 to 6
- gain: float32 [5120], replicated, may hold values from 0.1 to 1.9
Outputs:
- window_out: bfloat16 [128, 5120], P(('grp', 'seq')), parts along dimension 0
There are 2 independent parts, one for each index of `grp`. A program takes and returns all parts, laid end to end along the dimension named above; an argument that names none is the same for every part. Nothing has to cross between parts.
All inputs are finite; a program needn't handle non-finite values.
Results may differ from a plain program's by a relative error of at most 0.001.
Values may be sent and summed in bfloat16 or wider, within the bound.
A program may use at most 128 MiB of HBM per device.

v0:
```python
import math

import jax
import jax.numpy as jnp
from jax import lax
from jax.sharding import PartitionSpec as P

HEADS = 40
HDIM = 128


def split_groups(matrix):
    row_count = matrix.shape[0]
    group_count = HEADS // 8
    return matrix.reshape(row_count, group_count, 8, HDIM).transpose(1, 0, 2, 3)


def group_scores(query_part, key_part):
    score_scale = 1.0 / math.sqrt(HDIM)
    return (
        jnp.einsum("qhd,thd->hqt", query_part, key_part, preferred_element_type=jnp.float32)
        * score_scale
    )


def weighted_values(weights, value_part):
    return jnp.einsum(
        "hqt,thd->qhd", weights, value_part.astype(jnp.float32), precision=lax.Precision.HIGHEST
    )


def shards(queries, keys, values, gain):
    all_queries = lax.all_gather(queries, "seq", axis=0, tiled=True)
    window_rows = all_queries.shape[0]
    rows_here = queries.shape[0]
    query_groups = split_groups(all_queries)
    key_groups = split_groups(keys)
    value_groups = split_groups(values)

    def partial_of(members):
        query_part, key_part, value_part = members
        scores = group_scores(query_part, key_part)
        max_part = jnp.max(scores, axis=2)
        weights = jnp.exp(scores - max_part[:, :, None])
        return (weighted_values(weights, value_part), max_part, jnp.sum(weights, axis=2))

    numerator, local_max, denominator = lax.map(
        partial_of, (query_groups, key_groups, value_groups)
    )
    numer_rows = numerator.transpose(1, 0, 2, 3).reshape(window_rows, HEADS * HDIM)
    max_rows = local_max.reshape(HEADS, window_rows).transpose(1, 0)
    denom_rows = denominator.reshape(HEADS, window_rows).transpose(1, 0)
    numer_in, max_in, denom_in = (
        lax.all_to_all(numer_rows, "seq", split_axis=0, concat_axis=0, tiled=True),
        lax.all_to_all(max_rows, "seq", split_axis=0, concat_axis=0, tiled=True),
        lax.all_to_all(denom_rows, "seq", split_axis=0, concat_axis=0, tiled=True),
    )
    peer_count = lax.axis_size("seq")
    numer_in = numer_in.reshape(peer_count, rows_here, HEADS, HDIM)
    max_in = max_in.reshape(peer_count, rows_here, HEADS)
    denom_in = denom_in.reshape(peer_count, rows_here, HEADS)
    row_peak = jnp.max(max_in, axis=0)
    rescale = jnp.exp(max_in - row_peak[None])
    total_denom = jnp.sum(rescale * denom_in, axis=0)
    summed = jnp.sum(rescale[:, :, :, None] * numer_in, axis=0)
    attended = summed / total_denom[:, :, None]
    flattened = attended.reshape(rows_here, HEADS * HDIM)
    root_mean = jnp.sqrt(jnp.mean(flattened * flattened, axis=1, keepdims=True) + 1e-06)
    return (flattened / root_mean * gain).astype(jnp.bfloat16)


def solution(mesh):
    in_specs = (P(("grp", "seq"), None), P(("grp", "seq"), None), P(("grp", "seq"), None), P())
    out_specs = P(("grp", "seq"), None)
    return jax.shard_map(shards, mesh=mesh, in_specs=in_specs, out_specs=out_specs, check_vma=False)
```

profile of v0, /device:TPU:13, one launch (start us, length us, event | category | flops | bytes accessed | tf_op | source)
XLA Modules:
  0.0 119.3 jit_solution(9282598131096698049)
XLA Ops:
  0.0 7.9 %copy.23 = bf16[512,5120]{0,1:T(8,128)(2,1)} copy(bf16[512,5120]{1,0:T(8,128)(2,1)} %param.7) | data formatting | bytes 10485760 | tf_op args[1]
  7.9 0.0 copy-start
  7.9 8.0 %copy.22 = bf16[512,5120]{0,1:T(8,128)(2,1)} copy(bf16[512,5120]{1,0:T(8,128)(2,1)} %param.8) | data formatting | bytes 10485760 | tf_op args[2]
  15.9 0.0 copy-done
  15.9 17.4 %all-gather = bf16[16,4,5120]{2,1,0:T(4,128)(2,1)S(1)} all-gather(bf16[1,4,5120]{2,1,0:T(4,128)(2,1)S(1)} %bitcast.75), channel_id=1, replica_groups=mesh['grp'=2,'seq'=16] {'seq'}, dimensions={0}, use_global_device_ids=true | all-gather | bytes 696320 | tf_op jit(solution)/shard_map/all_gather | solution.py:33
  33.3 0.2 reshape.56
  33.6 22.7 %while.14 = (s32[]{:T(128)}, f32[5,64,8,128]{3,1,2,0:T(8,128)S(1)}, f32[5,8,64]{2,1,0:T(8,128)S(1)}, f32[5,8,64]{2,1,0:T(8,128)S(1)}, bf16[5,512,8,128]{1,3,2,0:...) while((s32[]{:T(128)}, f32[5,64,8,128]{3,1,2,0:T(8,128)S(1)}, ...), condition=%wide.region_3.4_spmd, body=%wide.region_0.3_spmd.sunk | while | flops 471071744 | bytes 5926493 | solution.py:47
  33.6 1.6 %fusion.18 = (f32[8,64]{1,0:T(8,128)S(1)}, f32[8,64,512]{2,1,0:T(8,128)S(1)}) fusion(bf16[5,512,8,128]{1,3,2,0:T(8,128)(2,1)} %get-tuple-element.161, s32[]{:T(128)} %get-tuple-element.147, bf16[1,64,8,128]{3,2,0,1:T(8,128)(2,1)S(1)} %constant_dynamic-slice_fusion.2), kind=kOutput, calls=%fused_computation.27.clone.1 | convolution fusion | flops 67632640 | bytes 2230784 | tf_op jit(solution)/shard_map/while/body/eval_jaxpr/qhd,thd->hqt/dot_general | solution.py:21
  35.2 0.4 fusion.20
  35.6 2.5 %fusion.19 = f32[5,64,8,128]{3,1,2,0:T(8,128)S(1)} fusion(f32[5,64,8,128]{3,1,2,0:T(8,128)S(1)} %get-tuple-element.148, s32[]{:T(128)} %get-tuple-element.147, bf16[5,512,8,128]{1,3,2,0:T(8,128)(2,1)} %get-tuple-element.159, f32[8,64,512]{2,1,0:T(8,128)S(1)} %get-tuple-element.135, f32[8,64]{1,0:T(8,128)S(1)} %get-tuple-element.136), kind=kOutput, calls=%fused_computation.2.clone.1 | convolution fusion | flops 402915328 | bytes 2364416 | tf_op jit(solution)/shard_map/while/body/eval_jaxpr/hqt,thd->qhd/dot_general | solution.py:27
  38.1 1.6 %fusion.18 = (f32[8,64]{1,0:T(8,128)S(1)}, f32[8,64,512]{2,1,0:T(8,128)S(1)}) fusion(bf16[5,512,8,128]{1,3,2,0:T(8,128)(2,1)} %get-tuple-element.161, s32[]{:T(128)} %get-tuple-element.147, bf16[1,64,8,128]{3,2,0,1:T(8,128)(2,1)S(1)} %constant_dynamic-slice_fusion.2), kind=kOutput, calls=%fused_computation.27.clone.1 | convolution fusion | flops 67632640 | bytes 2230784 | tf_op jit(solution)/shard_map/while/body/eval_jaxpr/qhd,thd->hqt/dot_general | solution.py:21
  39.7 0.4 fusion.20
  40.1 2.5 %fusion.19 = f32[5,64,8,128]{3,1,2,0:T(8,128)S(1)} fusion(f32[5,64,8,128]{3,1,2,0:T(8,128)S(1)} %get-tuple-element.148, s32[]{:T(128)} %get-tuple-element.147, bf16[5,512,8,128]{1,3,2,0:T(8,128)(2,1)} %get-tuple-element.159, f32[8,64,512]{2,1,0:T(8,128)S(1)} %get-tuple-element.135, f32[8,64]{1,0:T(8,128)S(1)} %get-tuple-element.136), kind=kOutput, calls=%fused_computation.2.clone.1 | convolution fusion | flops 402915328 | bytes 2364416 | tf_op jit(solution)/shard_map/while/body/eval_jaxpr/hqt,thd->qhd/dot_general | solution.py:27
  42.7 1.6 %fusion.18 = (f32[8,64]{1,0:T(8,128)S(1)}, f32[8,64,512]{2,1,0:T(8,128)S(1)}) fusion(bf16[5,512,8,128]{1,3,2,0:T(8,128)(2,1)} %get-tuple-element.161, s32[]{:T(128)} %get-tuple-element.147, bf16[1,64,8,128]{3,2,0,1:T(8,128)(2,1)S(1)} %constant_dynamic-slice_fusion.2), kind=kOutput, calls=%fused_computation.27.clone.1 | convolution fusion | flops 67632640 | bytes 2230784 | tf_op jit(solution)/shard_map/while/body/eval_jaxpr/qhd,thd->hqt/dot_general | solution.py:21
  44.3 0.4 fusion.20
  44.7 2.5 %fusion.19 = f32[5,64,8,128]{3,1,2,0:T(8,128)S(1)} fusion(f32[5,64,8,128]{3,1,2,0:T(8,128)S(1)} %get-tuple-element.148, s32[]{:T(128)} %get-tuple-element.147, bf16[5,512,8,128]{1,3,2,0:T(8,128)(2,1)} %get-tuple-element.159, f32[8,64,512]{2,1,0:T(8,128)S(1)} %get-tuple-element.135, f32[8,64]{1,0:T(8,128)S(1)} %get-tuple-element.136), kind=kOutput, calls=%fused_computation.2.clone.1 | convolution fusion | flops 402915328 | bytes 2364416 | tf_op jit(solution)/shard_map/while/body/eval_jaxpr/hqt,thd->qhd/dot_general | solution.py:27
  47.2 1.6 %fusion.18 = (f32[8,64]{1,0:T(8,128)S(1)}, f32[8,64,512]{2,1,0:T(8,128)S(1)}) fusion(bf16[5,512,8,128]{1,3,2,0:T(8,128)(2,1)} %get-tuple-element.161, s32[]{:T(128)} %get-tuple-element.147, bf16[1,64,8,128]{3,2,0,1:T(8,128)(2,1)S(1)} %constant_dynamic-slice_fusion.2), kind=kOutput, calls=%fused_computation.27.clone.1 | convolution fusion | flops 67632640 | bytes 2230784 | tf_op jit(solution)/shard_map/while/body/eval_jaxpr/qhd,thd->hqt/dot_general | solution.py:21
  48.8 0.4 fusion.20
  49.2 2.5 %fusion.19 = f32[5,64,8,128]{3,1,2,0:T(8,128)S(1)} fusion(f32[5,64,8,128]{3,1,2,0:T(8,128)S(1)} %get-tuple-element.148, s32[]{:T(128)} %get-tuple-element.147, bf16[5,512,8,128]{1,3,2,0:T(8,128)(2,1)} %get-tuple-element.159, f32[8,64,512]{2,1,0:T(8,128)S(1)} %get-tuple-element.135, f32[8,64]{1,0:T(8,128)S(1)} %get-tuple-element.136), kind=kOutput, calls=%fused_computation.2.clone.1 | convolution fusion | flops 402915328 | bytes 2364416 | tf_op jit(solution)/shard_map/while/body/eval_jaxpr/hqt,thd->qhd/dot_general | solution.py:27
  51.7 1.6 %fusion.18 = (f32[8,64]{1,0:T(8,128)S(1)}, f32[8,64,512]{2,1,0:T(8,128)S(1)}) fusion(bf16[5,512,8,128]{1,3,2,0:T(8,128)(2,1)} %get-tuple-element.161, s32[]{:T(128)} %get-tuple-element.147, bf16[1,64,8,128]{3,2,0,1:T(8,128)(2,1)S(1)} %constant_dynamic-slice_fusion.2), kind=kOutput, calls=%fused_computation.27.clone.1 | convolution fusion | flops 67632640 | bytes 2230784 | tf_op jit(solution)/shard_map/while/body/eval_jaxpr/qhd,thd->hqt/dot_general | solution.py:21
  53.4 0.4 fusion.20
  53.7 2.5 %fusion.19 = f32[5,64,8,128]{3,1,2,0:T(8,128)S(1)} fusion(f32[5,64,8,128]{3,1,2,0:T(8,128)S(1)} %get-tuple-element.148, s32[]{:T(128)} %get-tuple-element.147, bf16[5,512,8,128]{1,3,2,0:T(8,128)(2,1)} %get-tuple-element.159, f32[8,64,512]{2,1,0:T(8,128)S(1)} %get-tuple-element.135, f32[8,64]{1,0:T(8,128)S(1)} %get-tuple-element.136), kind=kOutput, calls=%fused_computation.2.clone.1 | convolution fusion | flops 402915328 | bytes 2364416 | tf_op jit(solution)/shard_map/while/body/eval_jaxpr/hqt,thd->qhd/dot_general | solution.py:27
  56.2 0.1 copy.27
  56.3 0.7 reshape.63
  57.0 10.2 %all-to-all-start = ((f32[16,1,160]{2,1,0:T(1,128)}), f32[16,1,160]{2,1,0:T(1,128)S(1)}, u32[]{:S(2)}, u32[]{:S(2)}) async-start(f32[16,1,160]{2,1,0:T(1,128)} %reshape.63), calls=%async_computation | async-start | bytes 32768 | tf_op jit(solution)/shard_map/all_to_all | solution.py:55
  67.3 0.1 copy.29
  67.3 0.7 reshape.65
  68.1 3.4 %all-to-all-done = f32[16,1,160]{2,1,0:T(1,128)S(1)} async-done(((f32[16,1,160]{2,1,0:T(1,128)}), f32[16,1,160]{2,1,0:T(1,128)S(1)}, u32[]{:S(2)}, u32[]{:S(2)}) %all-to-all-start) | async-done | bytes 10272 | tf_op jit(solution)/shard_map/all_to_all | solution.py:55
  71.4 5.8 %all-to-all-start.2 = ((f32[16,1,160]{2,1,0:T(1,128)}), f32[16,1,160]{2,1,0:T(1,128)S(1)}, u32[]{:S(2)}, u32[]{:S(2)}) async-start(f32[16,1,160]{2,1,0:T(1,128)} %reshape.65), calls=%async_computation.2 | async-start | bytes 32768 | tf_op jit(solution)/shard_map/all_to_all | solution.py:56
  77.2 0.8 copy.28
  78.0 1.5 %all_to_all.20 = f32[16,4,5120]{2,1,0:T(4,128)} reshape(f32[64,5,8,128]{3,2,1,0:T(8,128)S(1)} %copy.28) | data formatting | bytes 2621440 | tf_op jit(solution)/shard_map/all_to_all | solution.py:54
  79.5 1.9 %all-to-all-done.2 = f32[16,1,160]{2,1,0:T(1,128)S(1)} async-done(((f32[16,1,160]{2,1,0:T(1,128)}), f32[16,1,160]{2,1,0:T(1,128)S(1)}, u32[]{:S(2)}, u32[]{:S(2)}) %all-to-all-start.2) | async-done | bytes 10272 | tf_op jit(solution)/shard_map/all_to_all | solution.py:56
  81.4 6.0 %all-to-all-start.1 = ((f32[16,4,5120]{2,1,0:T(4,128)}), f32[16,4,5120]{2,1,0:T(4,128)S(1)}, u32[]{:S(2)}, u32[]{:S(2)}) async-start(f32[16,4,5120]{2,1,0:T(4,128)} %all_to_all.20), calls=%async_computation.1 | async-start | bytes 2621440 | tf_op jit(solution)/shard_map/all_to_all | solution.py:54
  87.4 0.5 broadcast.40
  87.9 0.7 reduce.7
  88.6 0.1 reshape.64
  88.7 0.7 reduce.6
  89.4 0.1 reshape.66
  89.5 1.5 %mul.32 = f32[16,4,40,128]{3,2,1,0:T(8,128)} broadcast(f32[16,4,40]{2,1,0:T(4,128)S(1)} %get-tuple-element.83), dimensions={0,1,2} | broadcast | bytes 1320960 | tf_op jit(solution)/shard_map/mul | solution.py:65
  91.0 1.7 %mul.33 = f32[16,4,5120]{2,1,0:T(4,128)S(1)} reshape(f32[16,4,40,128]{3,2,1,0:T(8,128)} %mul.32) | data formatting | bytes 2621440 | tf_op jit(solution)/shard_map/mul | solution.py:65
  92.8 0.1 broadcast_bitcast_fusion
  92.9 0.0 copy-start.1
  92.9 25.1 %all-to-all-done.1 = f32[16,4,5120]{2,1,0:T(4,128)S(1)} async-done(((f32[16,4,5120]{2,1,0:T(4,128)}), f32[16,4,5120]{2,1,0:T(4,128)S(1)}, u32[]{:S(2)}, u32[]{:S(2)}) %all-to-all-start.1) | async-done | bytes 1310752 | tf_op jit(solution)/shard_map/all_to_all | solution.py:54
  118.0 0.4 multiply_reduce_fusion
  118.4 0.2 fusion.11
  118.5 0.0 copy-done.1
  118.5 0.7 multiply_convert_fusion
  (16 shorter events, 0.2 us)
Async XLA Ops:
  7.9 8.0 %copy-start = (bf16[4,5120]{1,0:T(4,128)(2,1)S(1)}, bf16[4,5120]{1,0:T(4,128)(2,1)}, u32[]{:S(2)}) copy-start(bf16[4,5120]{1,0:T(4,128)(2,1)} %param.6) | copy-start | bytes 122884
  57.0 14.4 %all-to-all-start = ((f32[16,1,160]{2,1,0:T(1,128)}), f32[16,1,160]{2,1,0:T(1,128)S(1)}, u32[]{:S(2)}, u32[]{:S(2)}) async-start(f32[16,1,160]{2,1,0:T(1,128)} %reshape.63), calls=%async_computation | async-start | bytes 32768 | tf_op jit(solution)/shard_map/all_to_all | solution.py:55
  71.4 10.0 %all-to-all-start.2 = ((f32[16,1,160]{2,1,0:T(1,128)}), f32[16,1,160]{2,1,0:T(1,128)S(1)}, u32[]{:S(2)}, u32[]{:S(2)}) async-start(f32[16,1,160]{2,1,0:T(1,128)} %reshape.65), calls=%async_computation.2 | async-start | bytes 32768 | tf_op jit(solution)/shard_map/all_to_all | solution.py:56
  81.4 36.6 %all-to-all-start.1 = ((f32[16,4,5120]{2,1,0:T(4,128)}), f32[16,4,5120]{2,1,0:T(4,128)S(1)}, u32[]{:S(2)}, u32[]{:S(2)}) async-start(f32[16,4,5120]{2,1,0:T(4,128)} %all_to_all.20), calls=%async_computation.1 | async-start | bytes 2621440 | tf_op jit(solution)/shard_map/all_to_all | solution.py:54
  92.9 25.7 %copy-start.1 = (f32[5120]{0:T(1024)S(1)}, f32[5120]{0:T(1024)}, u32[]{:S(2)}) copy-start(f32[5120]{0:T(1024)} %param.9) | copy-start | bytes 61444
where the time goes:
time: 120 us; the launch traced here: 119 us
  waiting for transfers between devices  30.3 us (25%)
  local copies, waits for them, and re-layouts  24.1 us (20%)
  starting transfers between devices  22.1 us (18%)
  matrix products  20.5 us (17%)
  blocking collectives  17.4 us (14%)
  other arithmetic  4.56 us (4%)
    all_to_all x1, waiting for transfers between devices, shards(): lax.all_to_all(numer_rows, 'seq', split_axis=0, concat_axis=0, tiled=True)  25.1 us
    unnamed x11, local copies, waits for them, and re-layouts  17.6 us
    all_gather x1, blocking collectives, shards(): all_queries = lax.all_gather(queries, 'seq', axis=0, tiled=True)  17.4 us
    dot_general x5, matrix products, weighted_values(): jnp.einsum('hqt,thd->qhd', weights, value_part.astype(jnp.float32), preci...  12.5 us
    all_to_all x1, starting transfers between devices, shards(): lax.all_to_all(max_rows, 'seq', split_axis=0, concat_axis=0, tiled=True)  10.2 us
    dot_general x5, matrix products, group_scores(): jnp.einsum('qhd,thd->hqt', query_part, key_part, preferred_element_type=j...  8.02 us
    all_to_all x1, starting transfers between devices, shards(): lax.all_to_all(numer_rows, 'seq', split_axis=0, concat_axis=0, tiled=True)  6.02 us
    all_to_all x1, starting transfers between devices, shards(): lax.all_to_all(denom_rows, 'seq', split_axis=0, concat_axis=0, tiled=True)  5.81 us
  transfers between devices with their start and end apart: 3, of which 3 were waited for; matrix products, arithmetic and copies ran while one was open for 6% of the time, Pallas kernels for 0%

commit v1 on v0

v1 whole, which is shorter than its diff:
```python
import functools
import math

import jax
import jax.numpy as jnp
from jax import lax
from jax.experimental import pallas as pl
from jax.experimental.pallas import tpu as pltpu
from jax.sharding import PartitionSpec as P

HDIM = 128
CHUNKS = (2, 4, 4)


def chunk_sizes(quads):
    if sum(CHUNKS) == quads:
        return CHUNKS
    return (quads,)


def remote(src, dst, send_sem, recv_sem, peer):
    return pltpu.make_async_remote_copy(
        src_ref=src,
        dst_ref=dst,
        send_sem=send_sem,
        recv_sem=recv_sem,
        device_id={"seq": peer},
        device_id_type=pl.DeviceIdType.MESH,
    )


def merge(left, right, out, pairs):
    width = pairs * HDIM
    slots = out.shape[0]
    rows = slots * 8
    stat_l = left[:, :, width:].reshape(rows, HDIM)
    stat_r = right[:, :, width:].reshape(rows, HDIM)
    peak = jnp.maximum(stat_l, stat_r)
    scale_l = jnp.exp2(stat_l - peak)
    scale_r = jnp.exp2(stat_r - peak)
    total = stat_l * pltpu.roll(scale_l, 64, 1) + stat_r * pltpu.roll(scale_r, 64, 1)
    column = lax.broadcasted_iota(jnp.int32, (rows, HDIM), 1)
    out[:, :, width:] = jnp.where(column < 64, peak, total).reshape(slots, 8, HDIM)
    for pair in range(pairs):
        at = pl.ds(pair * HDIM, HDIM)
        part_l = left[:, :, at].reshape(rows, HDIM) * scale_l[:, pair : pair + 1]
        part_r = right[:, :, at].reshape(rows, HDIM) * scale_r[:, pair : pair + 1]
        out[:, :, at] = (part_l + part_r).reshape(slots, 8, HDIM)


def kernel(n, sizes, q_ref, k_hbm, v_hbm, gain_ref, o_ref, *scratch):
    count = len(sizes)
    scratch = list(scratch)

    def take(many):
        taken = scratch[:many]
        del scratch[:many]
        return taken

    part, from_core, to_y, from_y, own, from_z = (take(count) for _ in range(6))
    k_buf, v_buf, packed, q_all, attended = take(5)
    kv_sem, gz_send, gz_recv, gy_send, gy_recv, gc_send, gc_recv = take(7)
    c_send, c_recv, y_send, y_recv, z_send, z_recv = take(6)

    nz = n // 4
    me = lax.axis_index("seq")
    z, y, core = me // 4, lax.rem(me // 2, 2), lax.rem(me, 2)
    sibling = z * 4 + y * 2 + (1 - core)
    across = z * 4 + (1 - y) * 2 + core
    offsets = list(range(1, nz))

    def z_peer(step):
        return lax.rem(z + step, nz)

    def device_at(zz):
        return zz * 4 + y * 2 + core

    starts = [sum(sizes[:i]) for i in range(count)]

    loads = []
    for i in range(count):
        columns = pl.ds(starts[i] * 4 * HDIM, sizes[i] * 4 * HDIM)
        pair = []
        for which, (hbm, buf) in enumerate(((k_hbm, k_buf), (v_hbm, v_buf))):
            copy = pltpu.make_async_copy(
                hbm.at[:, columns], buf.at[:, columns], kv_sem.at[i, which]
            )
            copy.start()
            pair.append(copy)
        loads.append(pair)

    barrier = pltpu.get_barrier_semaphore()
    for peer in [sibling, across] + [device_at(z_peer(s)) for s in offsets]:
        pl.semaphore_signal(
            barrier, inc=1, device_id={"seq": peer}, device_id_type=pl.DeviceIdType.MESH
        )

    quads = sum(sizes)
    mine = q_ref[...].astype(jnp.float32)
    for quad in range(quads):
        for j in range(4):
            head = quad * 4 + j
            packed[4 * j : 4 * j + 4, quad * HDIM : (quad + 1) * HDIM] = mine[
                :, head * HDIM : (head + 1) * HDIM
            ]
    base = core * (2 * nz) + y * nz
    other_base = core * (2 * nz) + (1 - y) * nz
    q_all[base + z] = packed[...].astype(jnp.bfloat16)

    pl.semaphore_wait(barrier, nz - 1 + 2)

    own_block = q_all.at[base + z]
    sends = []
    for s in offsets:
        to = z_peer(s)
        copy = remote(own_block, own_block, gz_send.at[to], gz_recv.at[z], device_at(to))
        copy.start()
        sends.append(copy)
    copy = remote(own_block, own_block, gy_send.at[z], gy_recv.at[z], across)
    copy.start()
    sends.append(copy)
    for s in offsets:
        src = z_peer(s)
        block = q_all.at[base + src]
        remote(block, block, gz_send.at[src], gz_recv.at[src], device_at(src)).wait_recv()
        copy = remote(block, block, gy_send.at[src], gy_recv.at[src], across)
        copy.start()
        sends.append(copy)
    near = q_all.at[pl.ds(base, nz)]
    copy = remote(near, near, gc_send.at[0], gc_recv.at[0], sibling)
    copy.start()
    sends.append(copy)
    for s in [0] + offsets:
        src = z_peer(s)
        block = q_all.at[other_base + src]
        remote(block, block, gy_send.at[src], gy_recv.at[src], across).wait_recv()
    far = q_all.at[pl.ds(other_base, nz)]
    copy = remote(far, far, gc_send.at[1], gc_recv.at[1], sibling)
    copy.start()
    sends.append(copy)
    sib_base = (1 - core) * (2 * nz)
    sib_near = q_all.at[pl.ds(sib_base + y * nz, nz)]
    sib_far = q_all.at[pl.ds(sib_base + (1 - y) * nz, nz)]
    remote(sib_near, sib_near, gc_send.at[0], gc_recv.at[0], sibling).wait_recv()
    remote(sib_far, sib_far, gc_send.at[1], gc_recv.at[1], sibling).wait_recv()

    rows = n * 8
    log_scale = math.log2(math.e) / math.sqrt(HDIM)
    first = lax.rem(lax.broadcasted_iota(jnp.int32, (rows, HDIM), 0), 8) < 4
    column = lax.broadcasted_iota(jnp.int32, (rows, HDIM), 1)

    def compute(i):
        for copy in loads[i]:
            copy.wait()
        width = sizes[i] * 2 * HDIM
        out = part[i]

        def quad_step(step, stats):
            quad = starts[i] + step
            q_quad = q_all[:, :, pl.ds(pl.multiple_of(quad * HDIM, HDIM), HDIM)].astype(jnp.float32)
            for half in range(2):
                q_pair = q_quad[:, 8 * half : 8 * half + 8, :].reshape(rows, HDIM)
                spread = jnp.concatenate(
                    [jnp.where(first, q_pair, 0.0), jnp.where(first, 0.0, q_pair)], axis=1
                ).astype(jnp.bfloat16)
                at = pl.ds(pl.multiple_of(quad * 4 * HDIM + half * 2 * HDIM, 2 * HDIM), 2 * HDIM)
                scores = lax.dot_general(
                    spread, k_buf[:, at], (((1,), (1,)), ((), ())),
                    preferred_element_type=jnp.float32,
                )
                peak = jnp.max(scores, axis=1, keepdims=True) * log_scale
                weights = jnp.exp2(scores * log_scale - peak)
                total = jnp.sum(weights, axis=1, keepdims=True)
                high = weights.astype(jnp.bfloat16)
                low = (weights - high.astype(jnp.float32)).astype(jnp.bfloat16)
                both = jnp.dot(
                    jnp.concatenate([high, low], axis=0), v_buf[:, at],
                    preferred_element_type=jnp.float32,
                )
                summed = both[:rows] + both[rows:]
                picked = jnp.where(first, summed[:, :HDIM], summed[:, HDIM:])
                pair = step * 2 + half
                out[:, :, pl.ds(pl.multiple_of(pair * HDIM, HDIM), HDIM)] = picked.reshape(n, 8, HDIM)
                stats = jnp.where(column == pair, peak, stats)
                stats = jnp.where(column == pair + 64, total, stats)
            return stats

        stats = lax.fori_loop(0, sizes[i], quad_step, jnp.zeros((rows, HDIM), jnp.float32))
        out[:, :, width:] = stats.reshape(n, 8, HDIM)

    def start_core(i):
        copy = remote(
            part[i].at[pl.ds((1 - core) * (2 * nz), 2 * nz)], from_core[i],
            c_send.at[i], c_recv.at[i], sibling,
        )
        copy.start()
        return copy

    def start_y(i, core_copy):
        core_copy.wait_recv()
        pairs = sizes[i] * 2
        merge(
            part[i].at[pl.ds(other_base, nz)], from_core[i].at[pl.ds((1 - y) * nz, nz)], to_y[i], pairs
        )
        copy = remote(to_y[i], from_y[i], y_send.at[i], y_recv.at[i], across)
        copy.start()
        merge(part[i].at[pl.ds(base, nz)], from_core[i].at[pl.ds(y * nz, nz)], own[i], pairs)
        return copy

    to_z = part

    def start_z(i, y_copy, core_copy):
        y_copy.wait_recv()
        core_copy.wait_send()
        there = (1 - core) * (2 * nz)
        merge(own[i], from_y[i], to_z[i].at[pl.ds(there, nz)], sizes[i] * 2)
        copies = []
        for s in offsets:
            to = z_peer(s)
            copy = remote(
                to_z[i].at[there + to], from_z[i].at[z], z_send.at[i, to], z_recv.at[i, z], device_at(to)
            )
            copy.start()
            copies.append(copy)
        from_z[i][z] = to_z[i][there + z]
        return copies

    def finish(i):
        pairs = sizes[i] * 2
        width = pairs * HDIM
        for s in offsets:
            src = z_peer(s)
            remote(
                from_z[i].at[src], from_z[i].at[src], z_send.at[i, src], z_recv.at[i, src], device_at(src)
            ).wait_recv()
        stats = from_z[i][:, :, width:]
        peak = jnp.max(stats, axis=0)
        scales = [jnp.exp2(stats[k] - peak) for k in range(nz)]
        total = sum(stats[k] * pltpu.roll(scales[k], 64, 1) for k in range(nz))
        squares = jnp.zeros((8, HDIM), jnp.float32)
        for pair in range(pairs):
            at = pl.ds(pair * HDIM, HDIM)
            numer = sum(from_z[i][k, :, at] * scales[k][:, pair : pair + 1] for k in range(nz))
            value = numer / total[:, 64 + pair : 65 + pair]
            attended[:, pl.ds((starts[i] * 2 + pair) * HDIM, HDIM)] = value
            squares = squares + value * value
        return squares

    core_copies, y_copies, z_copies = [], [], []
    for i in range(count + 2):
        if i < count:
            compute(i)
            core_copies.append(start_core(i))
        if 0 <= i - 1 < count:
            y_copies.append(start_y(i - 1, core_copies[i - 1]))
        if 0 <= i - 2 < count:
            z_copies.append(start_z(i - 2, y_copies[i - 2], core_copies[i - 2]))

    squares = sum(finish(i) for i in range(count))
    squares = squares + pltpu.roll(squares, 4, 0)
    mean = jnp.sum(squares, axis=1, keepdims=True) * (1.0 / o_ref.shape[1])
    inverse = 1.0 / jnp.sqrt(mean + 1e-06)
    for pair in range(quads * 2):
        value = attended[:, pair * HDIM : (pair + 1) * HDIM] * inverse
        for j in range(2):
            at = pl.ds((pair * 2 + j) * HDIM, HDIM)
            o_ref[:, at] = (value[4 * j : 4 * j + 4] * gain_ref[:, at]).astype(jnp.bfloat16)

    for copy in sends + y_copies:
        copy.wait_send()
    for copies in z_copies:
        for copy in copies:
            copy.wait_send()


def shards(n, queries, keys, values, gain):
    rows_here, width = queries.shape
    tokens = keys.shape[0]
    quads = width // (4 * HDIM)
    sizes = chunk_sizes(quads)
    count = len(sizes)
    nz = n // 4
    wides = [(2 * size + 1) * HDIM for size in sizes]

    def per_chunk(slots):
        return [pltpu.VMEM((slots, 8, wide), jnp.float32) for wide in wides]

    dma = pltpu.SemaphoreType.DMA
    scratch = (
        per_chunk(n) + per_chunk(n // 2) + per_chunk(nz) + per_chunk(nz) + per_chunk(nz) + per_chunk(nz)
        + [
            pltpu.VMEM((tokens, width), jnp.bfloat16),
            pltpu.VMEM((tokens, width), jnp.bfloat16),
            pltpu.VMEM((16, quads * HDIM), jnp.float32),
            pltpu.VMEM((n, 16, quads * HDIM), jnp.bfloat16),
            pltpu.VMEM((8, quads * 2 * HDIM), jnp.float32),
        ]
        + [dma((count, 2)), dma((nz,)), dma((nz,)), dma((nz,)), dma((nz,)), dma((2,)), dma((2,))]
        + [dma((count,)), dma((count,)), dma((count,)), dma((count,)), dma((count, nz)), dma((count, nz))]
    )
    vmem = pl.BlockSpec(memory_space=pltpu.VMEM)
    hbm = pl.BlockSpec(memory_space=pltpu.HBM)
    return pl.pallas_call(
        functools.partial(kernel, n, sizes),
        out_shape=jax.ShapeDtypeStruct((rows_here, width), jnp.bfloat16),
        in_specs=[vmem, hbm, hbm, vmem],
        out_specs=vmem,
        scratch_shapes=scratch,
        compiler_params=pltpu.CompilerParams(
            collective_id=0, has_side_effects=True, vmem_limit_bytes=56 * 1024 * 1024
        ),
    )(queries, keys, values, gain.reshape(1, width))


def solution(mesh):
    n = mesh.shape["seq"]
    in_specs = (P(("grp", "seq"), None), P(("grp", "seq"), None), P(("grp", "seq"), None), P())
    out_specs = P(("grp", "seq"), None)
    return jax.shard_map(
        functools.partial(shards, n), mesh=mesh, in_specs=in_specs, out_specs=out_specs, check_vma=False
    )
```

time: 120 us -> 38.5 us (0.32)
  the two profiles are of different devices: /device:TPU:13 before, /device:TPU:0 now
where the time goes in v1:
time: 38.5 us; the launch traced here: 38.3 us
  Pallas kernels  36.8 us (96%)
  local copies, waits for them, and re-layouts  1.41 us (4%)
    pallas_call x1, Pallas kernels, shards(): pl.pallas_call(functools.partial(kernel, n, sizes), out_shape=jax.ShapeDt...  36.8 us
    unnamed x1, local copies, waits for them, and re-layouts  1.41 us

profile of v1, /device:TPU:0, one launch (start us, length us, event | category | flops | bytes accessed | tf_op | source)
XLA Modules:
  0.0 38.3 jit_solution(8907199974819257631)
XLA Ops:
  0.0 36.8 %shard_map.46 = bf16[4,5120]{1,0:T(4,128)(2,1)} custom-call(bf16[4,5120]{1,0:T(4,128)(2,1)} %q_ref.1, bf16[512,5120]{1,0:T(8,128)(2,1)} %k_hbm.1, bf16[512,5120]{1,0:T(8,128)(2,1)} %v_hbm.1, f32[1,5120]{1,0:T(1,128)} %bitcast.1), custom_call_target="tpu_custom_call" | custom-call | tf_op jit(solution)/shard_map/pallas_call | solution.py:303
  36.9 1.4 %copy.6 = bf16[4,5120]{1,0:T(4,128)(2,1)} copy(bf16[4,5120]{1,0:T(4,128)(2,1)} %shard_map.46) | data formatting | bytes 81920

commit v2 on v1

--- a/solution.py
+++ b/solution.py
@@ -9,7 +9,7 @@
 from jax.sharding import PartitionSpec as P
 
 HDIM = 128
-CHUNKS = (2, 4, 4)
+CHUNKS = (2, 3, 3, 2)
 
 
 def chunk_sizes(quads):
@@ -157,13 +157,13 @@
 
         def quad_step(step, stats):
             quad = starts[i] + step
-            q_quad = q_all[:, :, pl.ds(pl.multiple_of(quad * HDIM, HDIM), HDIM)].astype(jnp.float32)
+            q_quad = q_all[:, :, pl.ds(quad * HDIM, HDIM)].astype(jnp.float32)
             for half in range(2):
                 q_pair = q_quad[:, 8 * half : 8 * half + 8, :].reshape(rows, HDIM)
                 spread = jnp.concatenate(
                     [jnp.where(first, q_pair, 0.0), jnp.where(first, 0.0, q_pair)], axis=1
                 ).astype(jnp.bfloat16)
-                at = pl.ds(pl.multiple_of(quad * 4 * HDIM + half * 2 * HDIM, 2 * HDIM), 2 * HDIM)
+                at = pl.ds((quad * 2 + half) * 2 * HDIM, 2 * HDIM)
                 scores = lax.dot_general(
                     spread, k_buf[:, at], (((1,), (1,)), ((), ())),
                     preferred_element_type=jnp.float32,
@@ -180,12 +180,14 @@
                 summed = both[:rows] + both[rows:]
                 picked = jnp.where(first, summed[:, :HDIM], summed[:, HDIM:])
                 pair = step * 2 + half
-                out[:, :, pl.ds(pl.multiple_of(pair * HDIM, HDIM), HDIM)] = picked.reshape(n, 8, HDIM)
+                out[:, :, pl.ds(pair * HDIM, HDIM)] = picked.reshape(n, 8, HDIM)
                 stats = jnp.where(column == pair, peak, stats)
                 stats = jnp.where(column == pair + 64, total, stats)
             return stats
 
-        stats = lax.fori_loop(0, sizes[i], quad_step, jnp.zeros((rows, HDIM), jnp.float32))
+        stats = jnp.zeros((rows, HDIM), jnp.float32)
+        for step in range(sizes[i]):
+            stats = quad_step(step, stats)
         out[:, :, width:] = stats.reshape(n, 8, HDIM)
 
     def start_core(i):

time: 38.5 us -> 37.3 us (0.969)
  Pallas kernels: 36.8 us -> 35.7 us
    pallas_call x1, Pallas kernels: 36.8 us -> 35.7 us  [shards(): pl.pallas_call(functools.partial(kernel, n, sizes), out_shape=jax.ShapeDt...]
where the time goes in v2:
time: 37.3 us; the launch traced here: 37.1 us
  Pallas kernels  35.7 us (96%)
  local copies, waits for them, and re-layouts  1.41 us (4%)
    pallas_call x1, Pallas kernels, shards(): pl.pallas_call(functools.partial(kernel, n, sizes), out_shape=jax.ShapeDt...  35.7 us
    unnamed x1, local copies, waits for them, and re-layouts  1.41 us

profile of v2, /device:TPU:0, one launch (start us, length us, event | category | flops | bytes accessed | tf_op | source)
XLA Modules:
  0.0 37.1 jit_solution(9643383479281643683)
XLA Ops:
  0.0 35.7 %shard_map.46 = bf16[4,5120]{1,0:T(4,128)(2,1)} custom-call(bf16[4,5120]{1,0:T(4,128)(2,1)} %q_ref.1, bf16[512,5120]{1,0:T(8,128)(2,1)} %k_hbm.1, bf16[512,5120]{1,0:T(8,128)(2,1)} %v_hbm.1, f32[1,5120]{1,0:T(1,128)} %bitcast.1), custom_call_target="tpu_custom_call" | custom-call | tf_op jit(solution)/shard_map/pallas_call | solution.py:305
  35.7 1.4 %copy.6 = bf16[4,5120]{1,0:T(4,128)(2,1)} copy(bf16[4,5120]{1,0:T(4,128)(2,1)} %shard_map.46) | data formatting | bytes 81920

commit v3 on v2

--- a/solution.py
+++ b/solution.py
@@ -109,47 +109,65 @@
 
     pl.semaphore_wait(barrier, nz - 1 + 2)
 
-    own_block = q_all.at[base + z]
     sends = []
-    for s in offsets:
-        to = z_peer(s)
-        copy = remote(own_block, own_block, gz_send.at[to], gz_recv.at[z], device_at(to))
+    sib_base = (1 - core) * (2 * nz)
+
+    def piece(i, first, slots=1):
+        return q_all.at[pl.ds(first, slots), :, pl.ds(starts[i] * HDIM, sizes[i] * HDIM)]
+
+    def send(*args):
+        copy = remote(*args)
         copy.start()
         sends.append(copy)
-    copy = remote(own_block, own_block, gy_send.at[z], gy_recv.at[z], across)
-    copy.start()
-    sends.append(copy)
-    for s in offsets:
-        src = z_peer(s)
-        block = q_all.at[base + src]
-        remote(block, block, gz_send.at[src], gz_recv.at[src], device_at(src)).wait_recv()
-        copy = remote(block, block, gy_send.at[src], gy_recv.at[src], across)
-        copy.start()
-        sends.append(copy)
-    near = q_all.at[pl.ds(base, nz)]
-    copy = remote(near, near, gc_send.at[0], gc_recv.at[0], sibling)
-    copy.start()
-    sends.append(copy)
-    for s in [0] + offsets:
-        src = z_peer(s)
-        block = q_all.at[other_base + src]
-        remote(block, block, gy_send.at[src], gy_recv.at[src], across).wait_recv()
-    far = q_all.at[pl.ds(other_base, nz)]
-    copy = remote(far, far, gc_send.at[1], gc_recv.at[1], sibling)
-    copy.start()
-    sends.append(copy)
-    sib_base = (1 - core) * (2 * nz)
-    sib_near = q_all.at[pl.ds(sib_base + y * nz, nz)]
-    sib_far = q_all.at[pl.ds(sib_base + (1 - y) * nz, nz)]
-    remote(sib_near, sib_near, gc_send.at[0], gc_recv.at[0], sibling).wait_recv()
-    remote(sib_far, sib_far, gc_send.at[1], gc_recv.at[1], sibling).wait_recv()
+
+    def gather_z(i):
+        block = piece(i, base + z)
+        for s in offsets:
+            to = z_peer(s)
+            send(block, block, gz_send.at[i, to], gz_recv.at[i, z], device_at(to))
+
+    def gather_own(i):
+        block = piece(i, base + z)
+        send(block, block, gy_send.at[i, z], gy_recv.at[i, z], across)
+
+    def gather_y(i):
+        for s in offsets:
+            src = z_peer(s)
+            block = piece(i, base + src)
+            remote(block, block, gz_send.at[i, src], gz_recv.at[i, src], device_at(src)).wait_recv()
+            send(block, block, gy_send.at[i, src], gy_recv.at[i, src], across)
+        near = piece(i, base, nz)
+        send(near, near, gc_send.at[i, 0], gc_recv.at[i, 0], sibling)
+
+    def gather_core(i):
+        for s in [0] + offsets:
+            src = z_peer(s)
+            block = piece(i, other_base + src)
+            remote(block, block, gy_send.at[i, src], gy_recv.at[i, src], across).wait_recv()
+        far = piece(i, other_base, nz)
+        send(far, far, gc_send.at[i, 1], gc_recv.at[i, 1], sibling)
+
+    def gather_end(i):
+        near = piece(i, sib_base + y * nz, nz)
+        far = piece(i, sib_base + (1 - y) * nz, nz)
+        remote(near, near, gc_send.at[i, 0], gc_recv.at[i, 0], sibling).wait_recv()
+        remote(far, far, gc_send.at[i, 1], gc_recv.at[i, 1], sibling).wait_recv()
+
+    gather_z(0)
+    gather_own(0)
+    for i in range(1, count):
+        gather_z(i)
+    gather_y(0)
+    for i in range(1, count):
+        gather_own(i)
+    gather_core(0)
 
     rows = n * 8
     log_scale = math.log2(math.e) / math.sqrt(HDIM)
     first = lax.rem(lax.broadcasted_iota(jnp.int32, (rows, HDIM), 0), 8) < 4
     column = lax.broadcasted_iota(jnp.int32, (rows, HDIM), 1)
 
-    def compute(i):
+    def compute(i, middle):
         for copy in loads[i]:
             copy.wait()
         width = sizes[i] * 2 * HDIM
@@ -188,6 +206,8 @@
         stats = jnp.zeros((rows, HDIM), jnp.float32)
         for step in range(sizes[i]):
             stats = quad_step(step, stats)
+            if step == 0:
+                middle()
         out[:, :, width:] = stats.reshape(n, 8, HDIM)
 
     def start_core(i):
@@ -249,16 +269,31 @@
         return squares
 
     core_copies, y_copies, z_copies = [], [], []
-    for i in range(count + 2):
-        if i < count:
-            compute(i)
-            core_copies.append(start_core(i))
-        if 0 <= i - 1 < count:
+
+    def advance(i):
+        if i == 0:
+            for later in range(1, count):
+                gather_core(later)
+        if i >= 1:
             y_copies.append(start_y(i - 1, core_copies[i - 1]))
-        if 0 <= i - 2 < count:
+        if i >= 2:
             z_copies.append(start_z(i - 2, y_copies[i - 2], core_copies[i - 2]))
 
-    squares = sum(finish(i) for i in range(count))
+    for i in range(count):
+        gather_end(i)
+        if i == 0:
+            for later in range(1, count):
+                gather_y(later)
+        compute(i, functools.partial(advance, i))
+        core_copies.append(start_core(i))
+    squares = jnp.zeros((8, HDIM), jnp.float32)
+    for i in range(count - 2):
+        squares += finish(i)
+    y_copies.append(start_y(count - 1, core_copies[-1]))
+    for i in range(max(count - 2, 0), count):
+        z_copies.append(start_z(i, y_copies[i], core_copies[i]))
+    for i in range(max(count - 2, 0), count):
+        squares += finish(i)
     squares = squares + pltpu.roll(squares, 4, 0)
     mean = jnp.sum(squares, axis=1, keepdims=True) * (1.0 / o_ref.shape[1])
     inverse = 1.0 / jnp.sqrt(mean + 1e-06)
@@ -297,7 +332,7 @@
             pltpu.VMEM((n, 16, quads * HDIM), jnp.bfloat16),
             pltpu.VMEM((8, quads * 2 * HDIM), jnp.float32),
         ]
-        + [dma((count, 2)), dma((nz,)), dma((nz,)), dma((nz,)), dma((nz,)), dma((2,)), dma((2,))]
+        + [dma((count, 2))] + [dma((count, nz))] * 4 + [dma((count, 2))] * 2
         + [dma((count,)), dma((count,)), dma((count,)), dma((count,)), dma((count, nz)), dma((count, nz))]
     )
     vmem = pl.BlockSpec(memory_space=pltpu.VMEM)

time: 37.3 us -> 41.2 us (1.10)
  Pallas kernels: 35.7 us -> 39.5 us
    pallas_call x1, Pallas kernels: 35.7 us -> 39.5 us  [shards(): pl.pallas_call(functools.partial(kernel, n, sizes), out_shape=jax.ShapeDt...]
where the time goes in v3:
time: 41.2 us; the launch traced here: 40.9 us
  Pallas kernels  39.5 us (96%)
  local copies, waits for them, and re-layouts  1.41 us (3%)
    pallas_call x1, Pallas kernels, shards(): pl.pallas_call(functools.partial(kernel, n, sizes), out_shape=jax.ShapeDt...  39.5 us
    unnamed x1, local copies, waits for them, and re-layouts  1.41 us

profile of v3, /device:TPU:0, one launch (start us, length us, event | category | flops | bytes accessed | tf_op | source)
XLA Modules:
  0.0 40.9 jit_solution(11772406877663671145)
XLA Ops:
  0.0 39.5 %shard_map.46 = bf16[4,5120]{1,0:T(4,128)(2,1)} custom-call(bf16[4,5120]{1,0:T(4,128)(2,1)} %q_ref.1, bf16[512,5120]{1,0:T(8,128)(2,1)} %k_hbm.1, bf16[512,5120]{1,0:T(8,128)(2,1)} %v_hbm.1, f32[1,5120]{1,0:T(1,128)} %bitcast.1), custom_call_target="tpu_custom_call" | custom-call | tf_op jit(solution)/shard_map/pallas_call | solution.py:340
  39.5 1.4 %copy.6 = bf16[4,5120]{1,0:T(4,128)(2,1)} copy(bf16[4,5120]{1,0:T(4,128)(2,1)} %shard_map.46) | data formatting | bytes 81920

commit v4 on v2

v4 whole, which is shorter than its diff:
```python
import functools
import math

import jax
import jax.numpy as jnp
from jax import lax
from jax.experimental import pallas as pl
from jax.experimental.pallas import tpu as pltpu
from jax.sharding import PartitionSpec as P

HDIM = 128
CHUNK_QUADS = 2


def remote(src, dst, send_sem, recv_sem, peer):
    return pltpu.make_async_remote_copy(
        src_ref=src,
        dst_ref=dst,
        send_sem=send_sem,
        recv_sem=recv_sem,
        device_id={"seq": peer},
        device_id_type=pl.DeviceIdType.MESH,
    )


def merge(left, right, out, pairs):
    width = pairs * HDIM
    slots = out.shape[0]
    rows = slots * 8
    stat_l = left[:, :, width:].reshape(rows, HDIM)
    stat_r = right[:, :, width:].reshape(rows, HDIM)
    peak = jnp.maximum(stat_l, stat_r)
    scale_l = jnp.exp2(stat_l - peak)
    scale_r = jnp.exp2(stat_r - peak)
    total = stat_l * pltpu.roll(scale_l, 64, 1) + stat_r * pltpu.roll(scale_r, 64, 1)
    column = lax.broadcasted_iota(jnp.int32, (rows, HDIM), 1)
    out[:, :, width:] = jnp.where(column < 64, peak, total).reshape(slots, 8, HDIM)
    for pair in range(pairs):
        at = pl.ds(pair * HDIM, HDIM)
        part_l = left[:, :, at].reshape(rows, HDIM) * scale_l[:, pair : pair + 1]
        part_r = right[:, :, at].reshape(rows, HDIM) * scale_r[:, pair : pair + 1]
        out[:, :, at] = (part_l + part_r).reshape(slots, 8, HDIM)


def kernel(
    n, per, q_ref, k_hbm, v_hbm, gain_ref, o_ref,
    part, from_core, to_y, from_y, own, to_z, from_z, k_buf, v_buf, packed, q_all, attended,
    kv_sem, gz_send, gz_recv, gy_send, gy_recv, gc_send, gc_recv,
    c_send, c_recv, y_send, y_recv, z_send, z_recv,
):
    count = part.shape[0]
    quads = count * per
    pairs = per * 2
    width = pairs * HDIM
    nz = n // 4
    me = lax.axis_index("seq")
    z, y, core = me // 4, lax.rem(me // 2, 2), lax.rem(me, 2)
    sibling = z * 4 + y * 2 + (1 - core)
    across = z * 4 + (1 - y) * 2 + core
    offsets = list(range(1, nz))

    def z_peer(step):
        return lax.rem(z + step, nz)

    def device_at(zz):
        return zz * 4 + y * 2 + core

    def aligned(start, size):
        return pl.ds(pl.multiple_of(start, HDIM), size)

    def loads(c):
        columns = aligned(c * (per * 4 * HDIM), per * 4 * HDIM)
        return [
            pltpu.make_async_copy(hbm.at[:, columns], buf.at[:, columns], kv_sem.at[c, which])
            for which, (hbm, buf) in enumerate(((k_hbm, k_buf), (v_hbm, v_buf)))
        ]

    @pl.loop(0, count)
    def _(c):
        for copy in loads(c):
            copy.start()

    barrier = pltpu.get_barrier_semaphore()
    for peer in [sibling, across] + [device_at(z_peer(s)) for s in offsets]:
        pl.semaphore_signal(
            barrier, inc=1, device_id={"seq": peer}, device_id_type=pl.DeviceIdType.MESH
        )

    @pl.loop(0, quads)
    def _(quad):
        for j in range(4):
            block = q_ref[:, aligned((quad * 4 + j) * HDIM, HDIM)].astype(jnp.float32)
            packed[4 * j : 4 * j + 4, aligned(quad * HDIM, HDIM)] = block

    base = core * (2 * nz) + y * nz
    other_base = core * (2 * nz) + (1 - y) * nz
    q_all[base + z] = packed[...].astype(jnp.bfloat16)

    pl.semaphore_wait(barrier, nz - 1 + 2)

    own_block = q_all.at[base + z]
    sends = []
    for s in offsets:
        to = z_peer(s)
        copy = remote(own_block, own_block, gz_send.at[to], gz_recv.at[z], device_at(to))
        copy.start()
        sends.append(copy)
    copy = remote(own_block, own_block, gy_send.at[z], gy_recv.at[z], across)
    copy.start()
    sends.append(copy)
    for s in offsets:
        src = z_peer(s)
        block = q_all.at[base + src]
        remote(block, block, gz_send.at[src], gz_recv.at[src], device_at(src)).wait_recv()
        copy = remote(block, block, gy_send.at[src], gy_recv.at[src], across)
        copy.start()
        sends.append(copy)
    near = q_all.at[pl.ds(base, nz)]
    copy = remote(near, near, gc_send.at[0], gc_recv.at[0], sibling)
    copy.start()
    sends.append(copy)
    for s in [0] + offsets:
        src = z_peer(s)
        block = q_all.at[other_base + src]
        remote(block, block, gy_send.at[src], gy_recv.at[src], across).wait_recv()
    far = q_all.at[pl.ds(other_base, nz)]
    copy = remote(far, far, gc_send.at[1], gc_recv.at[1], sibling)
    copy.start()
    sends.append(copy)
    sib_base = (1 - core) * (2 * nz)
    sib_near = q_all.at[pl.ds(sib_base + y * nz, nz)]
    sib_far = q_all.at[pl.ds(sib_base + (1 - y) * nz, nz)]
    remote(sib_near, sib_near, gc_send.at[0], gc_recv.at[0], sibling).wait_recv()
    remote(sib_far, sib_far, gc_send.at[1], gc_recv.at[1], sibling).wait_recv()

    rows = n * 8
    log_scale = math.log2(math.e) / math.sqrt(HDIM)
    first = lax.rem(lax.broadcasted_iota(jnp.int32, (rows, HDIM), 0), 8) < 4
    column = lax.broadcasted_iota(jnp.int32, (rows, HDIM), 1)

    def compute(c):
        out = part.at[c]
        stats = jnp.zeros((rows, HDIM), jnp.float32)
        for step in range(per):
            quad = c * per + step
            q_quad = q_all[:, :, aligned(quad * HDIM, HDIM)].astype(jnp.float32)
            for half in range(2):
                q_pair = q_quad[:, 8 * half : 8 * half + 8, :].reshape(rows, HDIM)
                spread = jnp.concatenate(
                    [jnp.where(first, q_pair, 0.0), jnp.where(first, 0.0, q_pair)], axis=1
                ).astype(jnp.bfloat16)
                at = aligned((quad * 2 + half) * 2 * HDIM, 2 * HDIM)
                scores = lax.dot_general(
                    spread, k_buf[:, at], (((1,), (1,)), ((), ())),
                    preferred_element_type=jnp.float32,
                )
                peak = jnp.max(scores, axis=1, keepdims=True) * log_scale
                weights = jnp.exp2(scores * log_scale - peak)
                total = jnp.sum(weights, axis=1, keepdims=True)
                high = weights.astype(jnp.bfloat16)
                low = (weights - high.astype(jnp.float32)).astype(jnp.bfloat16)
                both = jnp.dot(
                    jnp.concatenate([high, low], axis=0), v_buf[:, at],
                    preferred_element_type=jnp.float32,
                )
                summed = both[:rows] + both[rows:]
                picked = jnp.where(first, summed[:, :HDIM], summed[:, HDIM:])
                pair = step * 2 + half
                out[:, :, pl.ds(pair * HDIM, HDIM)] = picked.reshape(n, 8, HDIM)
                stats = jnp.where(column == pair, peak, stats)
                stats = jnp.where(column == pair + 64, total, stats)
        out[:, :, width:] = stats.reshape(n, 8, HDIM)

    def core_copy(c):
        half = part.at[c, pl.ds((1 - core) * (2 * nz), 2 * nz)]
        return remote(half, from_core.at[c], c_send.at[c], c_recv.at[c], sibling)

    def y_copy(c):
        return remote(to_y.at[c], from_y.at[c], y_send.at[c], y_recv.at[c], across)

    def z_copy(c, s):
        to = z_peer(s)
        return remote(
            to_z.at[c, to], from_z.at[c, z], z_send.at[c, to], z_recv.at[c, z], device_at(to)
        )

    def z_arrival(c, s):
        src = z_peer(s)
        return remote(
            to_z.at[c, src], from_z.at[c, src], z_send.at[c, src], z_recv.at[c, src], device_at(src)
        )

    def start_y(c):
        core_copy(c).wait_recv()
        merge(
            part.at[c, pl.ds(other_base, nz)], from_core.at[c, pl.ds((1 - y) * nz, nz)], to_y.at[c], pairs
        )
        y_copy(c).start()
        merge(part.at[c, pl.ds(base, nz)], from_core.at[c, pl.ds(y * nz, nz)], own.at[c], pairs)

    def start_z(c):
        y_copy(c).wait_recv()
        merge(own.at[c], from_y.at[c], to_z.at[c], pairs)
        for s in offsets:
            z_copy(c, s).start()
        from_z[c, z] = to_z[c, z]

    def finish(c, squares):
        for s in offsets:
            z_arrival(c, s).wait_recv()
        stats = from_z[c, :, :, width:]
        peak = jnp.max(stats, axis=0)
        scales = [jnp.exp2(stats[k] - peak) for k in range(nz)]
        total = sum(stats[k] * pltpu.roll(scales[k], 64, 1) for k in range(nz))
        for pair in range(pairs):
            at = pl.ds(pair * HDIM, HDIM)
            numer = sum(from_z[c, k, :, at] * scales[k][:, pair : pair + 1] for k in range(nz))
            value = numer / total[:, 64 + pair : 65 + pair]
            attended[c, :, at] = value
            squares = squares + value * value
        return squares

    @pl.loop(0, count + 2)
    def _(c):
        @pl.when(c < count)
        def _():
            for copy in loads(c):
                copy.wait()
            compute(c)
            core_copy(c).start()

        @pl.when((c >= 1) & (c <= count))
        def _():
            start_y(c - 1)

        @pl.when(c >= 2)
        def _():
            start_z(c - 2)

    squares = lax.fori_loop(0, count, finish, jnp.zeros((8, HDIM), jnp.float32))
    squares = squares + pltpu.roll(squares, 4, 0)
    mean = jnp.sum(squares, axis=1, keepdims=True) * (1.0 / o_ref.shape[1])
    inverse = 1.0 / jnp.sqrt(mean + 1e-06)

    @pl.loop(0, count)
    def _(c):
        for pair in range(pairs):
            value = attended[c, :, pair * HDIM : (pair + 1) * HDIM] * inverse
            for j in range(2):
                at = aligned(((c * pairs + pair) * 2 + j) * HDIM, HDIM)
                o_ref[:, at] = (value[4 * j : 4 * j + 4] * gain_ref[:, at]).astype(jnp.bfloat16)
        core_copy(c).wait_send()
        y_copy(c).wait_send()
        for s in offsets:
            z_copy(c, s).wait_send()

    for copy in sends:
        copy.wait_send()


def shards(n, queries, keys, values, gain):
    rows_here, width = queries.shape
    tokens = keys.shape[0]
    quads = width // (4 * HDIM)
    per = CHUNK_QUADS if quads % CHUNK_QUADS == 0 else 1
    count = quads // per
    nz = n // 4
    wide = (2 * per + 1) * HDIM

    def per_chunk(slots):
        return pltpu.VMEM((count, slots, 8, wide), jnp.float32)

    dma = pltpu.SemaphoreType.DMA
    scratch = [per_chunk(n), per_chunk(n // 2)] + [per_chunk(nz)] * 5
    scratch += [
        pltpu.VMEM((tokens, width), jnp.bfloat16),
        pltpu.VMEM((tokens, width), jnp.bfloat16),
        pltpu.VMEM((16, quads * HDIM), jnp.float32),
        pltpu.VMEM((n, 16, quads * HDIM), jnp.bfloat16),
        pltpu.VMEM((count, 8, 2 * per * HDIM), jnp.float32),
    ]
    scratch += [dma((count, 2))] + [dma((nz,))] * 4 + [dma((2,))] * 2
    scratch += [dma((count,))] * 4 + [dma((count, nz))] * 2
    vmem = pl.BlockSpec(memory_space=pltpu.VMEM)
    hbm = pl.BlockSpec(memory_space=pltpu.HBM)
    return pl.pallas_call(
        functools.partial(kernel, n, per),
        out_shape=jax.ShapeDtypeStruct((rows_here, width), jnp.bfloat16),
        in_specs=[vmem, hbm, hbm, vmem],
        out_specs=vmem,
        scratch_shapes=scratch,
        compiler_params=pltpu.CompilerParams(
            collective_id=0, has_side_effects=True, vmem_limit_bytes=56 * 1024 * 1024
        ),
    )(queries, keys, values, gain.reshape(1, width))


def solution(mesh):
    n = mesh.shape["seq"]
    in_specs = (P(("grp", "seq"), None), P(("grp", "seq"), None), P(("grp", "seq"), None), P())
    out_specs = P(("grp", "seq"), None)
    return jax.shard_map(
        functools.partial(shards, n), mesh=mesh, in_specs=in_specs, out_specs=out_specs, check_vma=False
    )
```

time: 37.3 us -> 38.5 us (1.032)
  Pallas kernels: 35.7 us -> 36.9 us
    pallas_call x1, Pallas kernels: 35.7 us -> 36.9 us  [shards(): pl.pallas_call(functools.partial(kernel, n, per), out_shape=jax.ShapeDtyp...]
where the time goes in v4:
time: 38.5 us; the launch traced here: 38.3 us
  Pallas kernels  36.9 us (96%)
  local copies, waits for them, and re-layouts  1.41 us (4%)
    pallas_call x1, Pallas kernels, shards(): pl.pallas_call(functools.partial(kernel, n, per), out_shape=jax.ShapeDtyp...  36.9 us
    unnamed x1, local copies, waits for them, and re-layouts  1.41 us

profile of v4, /device:TPU:0, one launch (start us, length us, event | category | flops | bytes accessed | tf_op | source)
XLA Modules:
  0.0 38.3 jit_solution(8661085731342657928)
XLA Ops:
  0.0 36.9 %shard_map.46 = bf16[4,5120]{1,0:T(4,128)(2,1)} custom-call(bf16[4,5120]{1,0:T(4,128)(2,1)} %q_ref.1, bf16[512,5120]{1,0:T(8,128)(2,1)} %k_hbm.1, bf16[512,5120]{1,0:T(8,128)(2,1)} %v_hbm.1, f32[1,5120]{1,0:T(1,128)} %bitcast.1), custom_call_target="tpu_custom_call" | custom-call | tf_op jit(solution)/shard_map/pallas_call | solution.py:286
  36.9 1.4 %copy.6 = bf16[4,5120]{1,0:T(4,128)(2,1)} copy(bf16[4,5120]{1,0:T(4,128)(2,1)} %shard_map.46) | data formatting | bytes 81920

commit v5 on v4

--- a/solution.py
+++ b/solution.py
@@ -98,47 +98,80 @@
 
     pl.semaphore_wait(barrier, nz - 1 + 2)
 
-    own_block = q_all.at[base + z]
-    sends = []
-    for s in offsets:
-        to = z_peer(s)
-        copy = remote(own_block, own_block, gz_send.at[to], gz_recv.at[z], device_at(to))
-        copy.start()
-        sends.append(copy)
-    copy = remote(own_block, own_block, gy_send.at[z], gy_recv.at[z], across)
-    copy.start()
-    sends.append(copy)
-    for s in offsets:
+    early = min(2, count - 1) * per
+    sib_base = (1 - core) * (2 * nz)
+
+    def piece(i, first, slots=1):
+        columns = pl.ds(0, early * HDIM) if i == 0 else pl.ds(early * HDIM, (quads - early) * HDIM)
+        return q_all.at[pl.ds(first, slots), :, columns]
+
+    def gather_z(i, s):
+        block, to = piece(i, base + z), z_peer(s)
+        return remote(block, block, gz_send.at[i, to], gz_recv.at[i, z], device_at(to))
+
+    def gather_z_arrival(i, s):
         src = z_peer(s)
-        block = q_all.at[base + src]
-        remote(block, block, gz_send.at[src], gz_recv.at[src], device_at(src)).wait_recv()
-        copy = remote(block, block, gy_send.at[src], gy_recv.at[src], across)
-        copy.start()
-        sends.append(copy)
-    near = q_all.at[pl.ds(base, nz)]
-    copy = remote(near, near, gc_send.at[0], gc_recv.at[0], sibling)
-    copy.start()
-    sends.append(copy)
+        block = piece(i, base + src)
+        return remote(block, block, gz_send.at[i, src], gz_recv.at[i, src], device_at(src))
+
+    def gather_y(s):
+        src = z_peer(s)
+        block = piece(0, base + src)
+        return remote(block, block, gy_send.at[src], gy_recv.at[src], across)
+
+    def gather_y_arrival(s):
+        src = z_peer(s)
+        block = piece(0, other_base + src)
+        return remote(block, block, gy_send.at[src], gy_recv.at[src], across)
+
+    def gather_core(half):
+        block = piece(0, base if half == 0 else other_base, nz)
+        return remote(block, block, gc_send.at[half], gc_recv.at[half], sibling)
+
+    def gather_core_arrival(half):
+        block = piece(0, sib_base + (y if half == 0 else 1 - y) * nz, nz)
+        return remote(block, block, gc_send.at[half], gc_recv.at[half], sibling)
+
+    def late_y():
+        block = piece(1, base, nz)
+        return remote(block, block, gy_send.at[nz], gy_recv.at[nz], across)
+
+    def late_y_arrival():
+        block = piece(1, other_base, nz)
+        return remote(block, block, gy_send.at[nz], gy_recv.at[nz], across)
+
+    def late_core():
+        block = piece(1, core * (2 * nz), 2 * nz)
+        return remote(block, block, gc_send.at[2], gc_recv.at[2], sibling)
+
+    def late_core_arrival():
+        block = piece(1, sib_base, 2 * nz)
+        return remote(block, block, gc_send.at[2], gc_recv.at[2], sibling)
+
+    for s in offsets:
+        gather_z(0, s).start()
+    gather_y(0).start()
+    for s in offsets:
+        gather_z(1, s).start()
+    for s in offsets:
+        gather_z_arrival(0, s).wait_recv()
+        gather_y(s).start()
+    gather_core(0).start()
     for s in [0] + offsets:
-        src = z_peer(s)
-        block = q_all.at[other_base + src]
-        remote(block, block, gy_send.at[src], gy_recv.at[src], across).wait_recv()
-    far = q_all.at[pl.ds(other_base, nz)]
-    copy = remote(far, far, gc_send.at[1], gc_recv.at[1], sibling)
-    copy.start()
-    sends.append(copy)
-    sib_base = (1 - core) * (2 * nz)
-    sib_near = q_all.at[pl.ds(sib_base + y * nz, nz)]
-    sib_far = q_all.at[pl.ds(sib_base + (1 - y) * nz, nz)]
-    remote(sib_near, sib_near, gc_send.at[0], gc_recv.at[0], sibling).wait_recv()
-    remote(sib_far, sib_far, gc_send.at[1], gc_recv.at[1], sibling).wait_recv()
+        gather_y_arrival(s).wait_recv()
+    gather_core(1).start()
+    for s in offsets:
+        gather_z_arrival(1, s).wait_recv()
+    late_y().start()
+    for half in range(2):
+        gather_core_arrival(half).wait_recv()
 
     rows = n * 8
     log_scale = math.log2(math.e) / math.sqrt(HDIM)
     first = lax.rem(lax.broadcasted_iota(jnp.int32, (rows, HDIM), 0), 8) < 4
     column = lax.broadcasted_iota(jnp.int32, (rows, HDIM), 1)
 
-    def compute(c):
+    def compute(c, middle):
         out = part.at[c]
         stats = jnp.zeros((rows, HDIM), jnp.float32)
         for step in range(per):
@@ -169,6 +202,8 @@
                 out[:, :, pl.ds(pair * HDIM, HDIM)] = picked.reshape(n, 8, HDIM)
                 stats = jnp.where(column == pair, peak, stats)
                 stats = jnp.where(column == pair + 64, total, stats)
+            if step == 0:
+                middle(c)
         out[:, :, width:] = stats.reshape(n, 8, HDIM)
 
     def core_copy(c):
@@ -220,24 +255,37 @@
             squares = squares + value * value
         return squares
 
-    @pl.loop(0, count + 2)
-    def _(c):
-        @pl.when(c < count)
-        def _():
-            for copy in loads(c):
-                copy.wait()
-            compute(c)
-            core_copy(c).start()
-
-        @pl.when((c >= 1) & (c <= count))
+    def advance(c):
+        @pl.when(c >= 1)
         def _():
             start_y(c - 1)
 
-        @pl.when(c >= 2)
+        @pl.when(c >= 3)
         def _():
-            start_z(c - 2)
-
-    squares = lax.fori_loop(0, count, finish, jnp.zeros((8, HDIM), jnp.float32))
+            start_z(c - 3)
+
+        @pl.when(c == 1)
+        def _():
+            late_y_arrival().wait_recv()
+            late_core().start()
+
+    @pl.loop(0, count)
+    def _(c):
+        @pl.when(c == 2)
+        def _():
+            late_core_arrival().wait_recv()
+
+        for copy in loads(c):
+            copy.wait()
+        compute(c, advance)
+        core_copy(c).start()
+
+    start_z(count - 3)
+    start_y(count - 1)
+    start_z(count - 2)
+    squares = lax.fori_loop(0, count - 2, finish, jnp.zeros((8, HDIM), jnp.float32))
+    start_z(count - 1)
+    squares = lax.fori_loop(count - 2, count, finish, squares)
     squares = squares + pltpu.roll(squares, 4, 0)
     mean = jnp.sum(squares, axis=1, keepdims=True) * (1.0 / o_ref.shape[1])
     inverse = 1.0 / jnp.sqrt(mean + 1e-06)
@@ -254,7 +302,12 @@
         for s in offsets:
             z_copy(c, s).wait_send()
 
-    for copy in sends:
+    for s in offsets:
+        gather_z(0, s).wait_send()
+        gather_z(1, s).wait_send()
+    for s in [0] + offsets:
+        gather_y(s).wait_send()
+    for copy in (gather_core(0), gather_core(1), late_y(), late_core()):
         copy.wait_send()
 
 
@@ -279,7 +332,7 @@
         pltpu.VMEM((n, 16, quads * HDIM), jnp.bfloat16),
         pltpu.VMEM((count, 8, 2 * per * HDIM), jnp.float32),
     ]
-    scratch += [dma((count, 2))] + [dma((nz,))] * 4 + [dma((2,))] * 2
+    scratch += [dma((count, 2))] + [dma((2, nz))] * 2 + [dma((nz + 1,))] * 2 + [dma((3,))] * 2
     scratch += [dma((count,))] * 4 + [dma((count, nz))] * 2
     vmem = pl.BlockSpec(memory_space=pltpu.VMEM)
     hbm = pl.BlockSpec(memory_space=pltpu.HBM)

time: 38.5 us -> 38.6 us (level)
  no operation moved by 1% of the time
where the time goes in v5:
time: 38.6 us; the launch traced here: 38.4 us
  Pallas kernels  37 us (96%)
  local copies, waits for them, and re-layouts  1.41 us (4%)
    pallas_call x1, Pallas kernels, shards(): pl.pallas_call(functools.partial(kernel, n, per), out_shape=jax.ShapeDtyp...  37 us
    unnamed x1, local copies, waits for them, and re-layouts  1.41 us

profile of v5, /device:TPU:0, one launch (start us, length us, event | category | flops | bytes accessed | tf_op | source)
XLA Modules:
  0.0 38.4 jit_solution(16894933928552937485)
XLA Ops:
  0.0 37.0 %shard_map.46 = bf16[4,5120]{1,0:T(4,128)(2,1)} custom-call(bf16[4,5120]{1,0:T(4,128)(2,1)} %q_ref.1, bf16[512,5120]{1,0:T(8,128)(2,1)} %k_hbm.1, bf16[512,5120]{1,0:T(8,128)(2,1)} %v_hbm.1, f32[1,5120]{1,0:T(1,128)} %bitcast.1), custom_call_target="tpu_custom_call" | custom-call | tf_op jit(solution)/shard_map/pallas_call | solution.py:339
  37.0 1.4 %copy.6 = bf16[4,5120]{1,0:T(4,128)(2,1)} copy(bf16[4,5120]{1,0:T(4,128)(2,1)} %shard_map.46) | data formatting | bytes 81920

commit v6 on v5

--- a/solution.py
+++ b/solution.py
@@ -169,27 +169,27 @@
     rows = n * 8
     log_scale = math.log2(math.e) / math.sqrt(HDIM)
     first = lax.rem(lax.broadcasted_iota(jnp.int32, (rows, HDIM), 0), 8) < 4
-    column = lax.broadcasted_iota(jnp.int32, (rows, HDIM), 1)
+    first_lane = lax.rem(lax.broadcasted_iota(jnp.int32, (HDIM, rows), 1), 8) < 4
+    line = lax.broadcasted_iota(jnp.int32, (HDIM, rows), 0)
 
     def compute(c, middle):
         out = part.at[c]
-        stats = jnp.zeros((rows, HDIM), jnp.float32)
+        stats = jnp.zeros((HDIM, rows), jnp.float32)
         for step in range(per):
             quad = c * per + step
             q_quad = q_all[:, :, aligned(quad * HDIM, HDIM)].astype(jnp.float32)
             for half in range(2):
                 q_pair = q_quad[:, 8 * half : 8 * half + 8, :].reshape(rows, HDIM)
+                turned = q_pair.T
                 spread = jnp.concatenate(
-                    [jnp.where(first, q_pair, 0.0), jnp.where(first, 0.0, q_pair)], axis=1
+                    [jnp.where(first_lane, turned, 0.0), jnp.where(first_lane, 0.0, turned)], axis=0
                 ).astype(jnp.bfloat16)
                 at = aligned((quad * 2 + half) * 2 * HDIM, 2 * HDIM)
-                scores = lax.dot_general(
-                    spread, k_buf[:, at], (((1,), (1,)), ((), ())),
-                    preferred_element_type=jnp.float32,
-                )
-                peak = jnp.max(scores, axis=1, keepdims=True) * log_scale
+                scores = jnp.dot(k_buf[:, at], spread, preferred_element_type=jnp.float32)
+                peak = jnp.max(scores, axis=0, keepdims=True) * log_scale
                 weights = jnp.exp2(scores * log_scale - peak)
-                total = jnp.sum(weights, axis=1, keepdims=True)
+                total = jnp.sum(weights, axis=0, keepdims=True)
+                weights = weights.T
                 high = weights.astype(jnp.bfloat16)
                 low = (weights - high.astype(jnp.float32)).astype(jnp.bfloat16)
                 both = jnp.dot(
@@ -200,11 +200,11 @@
                 picked = jnp.where(first, summed[:, :HDIM], summed[:, HDIM:])
                 pair = step * 2 + half
                 out[:, :, pl.ds(pair * HDIM, HDIM)] = picked.reshape(n, 8, HDIM)
-                stats = jnp.where(column == pair, peak, stats)
-                stats = jnp.where(column == pair + 64, total, stats)
+                stats = jnp.where(line == pair, peak, stats)
+                stats = jnp.where(line == pair + 64, total, stats)
             if step == 0:
                 middle(c)
-        out[:, :, width:] = stats.reshape(n, 8, HDIM)
+        out[:, :, width:] = stats.T.reshape(n, 8, HDIM)
 
     def core_copy(c):
         half = part.at[c, pl.ds((1 - core) * (2 * nz), 2 * nz)]

time: 38.6 us -> 39.4 us (1.021)
  Pallas kernels: 37 us -> 37.7 us
    pallas_call x1, Pallas kernels: 37 us -> 37.7 us  [shards(): pl.pallas_call(functools.partial(kernel, n, per), out_shape=jax.ShapeDtyp...]
where the time goes in v6:
time: 39.4 us; the launch traced here: 39.1 us
  Pallas kernels  37.7 us (96%)
  local copies, waits for them, and re-layouts  1.41 us (4%)
    pallas_call x1, Pallas kernels, shards(): pl.pallas_call(functools.partial(kernel, n, per), out_shape=jax.ShapeDtyp...  37.7 us
    unnamed x1, local copies, waits for them, and re-layouts  1.41 us

profile of v6, /device:TPU:0, one launch (start us, length us, event | category | flops | bytes accessed | tf_op | source)
XLA Modules:
  0.0 39.1 jit_solution(8696838408141589261)
XLA Ops:
  0.0 37.7 %shard_map.46 = bf16[4,5120]{1,0:T(4,128)(2,1)} custom-call(bf16[4,5120]{1,0:T(4,128)(2,1)} %q_ref.1, bf16[512,5120]{1,0:T(8,128)(2,1)} %k_hbm.1, bf16[512,5120]{1,0:T(8,128)(2,1)} %v_hbm.1, f32[1,5120]{1,0:T(1,128)} %bitcast.1), custom_call_target="tpu_custom_call" | custom-call | tf_op jit(solution)/shard_map/pallas_call | solution.py:339
  37.7 1.4 %copy.6 = bf16[4,5120]{1,0:T(4,128)(2,1)} copy(bf16[4,5120]{1,0:T(4,128)(2,1)} %shard_map.46) | data formatting | bytes 81920

commit v7 on v5

--- a/solution.py
+++ b/solution.py
@@ -171,39 +171,46 @@
     first = lax.rem(lax.broadcasted_iota(jnp.int32, (rows, HDIM), 0), 8) < 4
     column = lax.broadcasted_iota(jnp.int32, (rows, HDIM), 1)
 
+    def pair_columns(c, pair):
+        return aligned((c * pairs + pair) * 2 * HDIM, 2 * HDIM)
+
     def compute(c, middle):
         out = part.at[c]
         stats = jnp.zeros((rows, HDIM), jnp.float32)
-        for step in range(per):
-            quad = c * per + step
+        scores = []
+        for pair in range(pairs):
+            quad = c * per + pair // 2
             q_quad = q_all[:, :, aligned(quad * HDIM, HDIM)].astype(jnp.float32)
-            for half in range(2):
-                q_pair = q_quad[:, 8 * half : 8 * half + 8, :].reshape(rows, HDIM)
-                spread = jnp.concatenate(
-                    [jnp.where(first, q_pair, 0.0), jnp.where(first, 0.0, q_pair)], axis=1
-                ).astype(jnp.bfloat16)
-                at = aligned((quad * 2 + half) * 2 * HDIM, 2 * HDIM)
-                scores = lax.dot_general(
-                    spread, k_buf[:, at], (((1,), (1,)), ((), ())),
+            half = pair % 2
+            q_pair = q_quad[:, 8 * half : 8 * half + 8, :].reshape(rows, HDIM)
+            spread = jnp.concatenate(
+                [jnp.where(first, q_pair, 0.0), jnp.where(first, 0.0, q_pair)], axis=1
+            ).astype(jnp.bfloat16)
+            scores.append(
+                lax.dot_general(
+                    spread, k_buf[:, pair_columns(c, pair)], (((1,), (1,)), ((), ())),
                     preferred_element_type=jnp.float32,
                 )
-                peak = jnp.max(scores, axis=1, keepdims=True) * log_scale
-                weights = jnp.exp2(scores * log_scale - peak)
-                total = jnp.sum(weights, axis=1, keepdims=True)
-                high = weights.astype(jnp.bfloat16)
-                low = (weights - high.astype(jnp.float32)).astype(jnp.bfloat16)
-                both = jnp.dot(
-                    jnp.concatenate([high, low], axis=0), v_buf[:, at],
-                    preferred_element_type=jnp.float32,
-                )
-                summed = both[:rows] + both[rows:]
-                picked = jnp.where(first, summed[:, :HDIM], summed[:, HDIM:])
-                pair = step * 2 + half
-                out[:, :, pl.ds(pair * HDIM, HDIM)] = picked.reshape(n, 8, HDIM)
-                stats = jnp.where(column == pair, peak, stats)
-                stats = jnp.where(column == pair + 64, total, stats)
-            if step == 0:
-                middle(c)
+            )
+        middle(c)
+        peaks = [jnp.max(score, axis=1, keepdims=True) * log_scale for score in scores]
+        weights = [jnp.exp2(score * log_scale - peak) for score, peak in zip(scores, peaks)]
+        split = []
+        for weight in weights:
+            high = weight.astype(jnp.bfloat16)
+            low = (weight - high.astype(jnp.float32)).astype(jnp.bfloat16)
+            split.append(jnp.concatenate([high, low], axis=0))
+        products = [
+            jnp.dot(split[pair], v_buf[:, pair_columns(c, pair)], preferred_element_type=jnp.float32)
+            for pair in range(pairs)
+        ]
+        totals = [jnp.sum(weight, axis=1, keepdims=True) for weight in weights]
+        for pair in range(pairs):
+            summed = products[pair][:rows] + products[pair][rows:]
+            picked = jnp.where(first, summed[:, :HDIM], summed[:, HDIM:])
+            out[:, :, pl.ds(pair * HDIM, HDIM)] = picked.reshape(n, 8, HDIM)
+            stats = jnp.where(column == pair, peaks[pair], stats)
+            stats = jnp.where(column == pair + 64, totals[pair], stats)
         out[:, :, width:] = stats.reshape(n, 8, HDIM)
 
     def core_copy(c):

time: 38.6 us -> 36.9 us (0.956)
  Pallas kernels: 37 us -> 35.2 us
    pallas_call x1, Pallas kernels: 37 us -> 35.2 us  [shards(): pl.pallas_call(functools.partial(kernel, n, per), out_shape=jax.ShapeDtyp...]
where the time goes in v7:
time: 36.9 us; the launch traced here: 36.7 us
  Pallas kernels  35.2 us (95%)
  local copies, waits for them, and re-layouts  1.41 us (4%)
    pallas_call x1, Pallas kernels, shards(): pl.pallas_call(functools.partial(kernel, n, per), out_shape=jax.ShapeDtyp...  35.2 us
    unnamed x1, local copies, waits for them, and re-layouts  1.41 us

profile of v7, /device:TPU:0, one launch (start us, length us, event | category | flops | bytes accessed | tf_op | source)
XLA Modules:
  0.0 36.7 jit_solution(10596013538576865905)
XLA Ops:
  0.0 35.2 %shard_map.46 = bf16[4,5120]{1,0:T(4,128)(2,1)} custom-call(bf16[4,5120]{1,0:T(4,128)(2,1)} %q_ref.1, bf16[512,5120]{1,0:T(8,128)(2,1)} %k_hbm.1, bf16[512,5120]{1,0:T(8,128)(2,1)} %v_hbm.1, f32[1,5120]{1,0:T(1,128)} %bitcast.1), custom_call_target="tpu_custom_call" | custom-call | tf_op jit(solution)/shard_map/pallas_call | solution.py:346
  35.3 1.4 %copy.6 = bf16[4,5120]{1,0:T(4,128)(2,1)} copy(bf16[4,5120]{1,0:T(4,128)(2,1)} %shard_map.46) | data formatting | bytes 81920

commit v8 on v7

--- a/solution.py
+++ b/solution.py
@@ -44,7 +44,7 @@
 
 def kernel(
     n, per, q_ref, k_hbm, v_hbm, gain_ref, o_ref,
-    part, from_core, to_y, from_y, own, to_z, from_z, k_buf, v_buf, packed, q_all, attended,
+    part, from_core, to_y, from_y, own, to_z, from_z, k_buf, v_buf, packed, q_all, attended, score_buf,
     kv_sem, gz_send, gz_recv, gy_send, gy_recv, gc_send, gc_recv,
     c_send, c_recv, y_send, y_recv, z_send, z_recv,
 ):
@@ -68,17 +68,15 @@
     def aligned(start, size):
         return pl.ds(pl.multiple_of(start, HDIM), size)
 
-    def loads(c):
+    def load(c, which):
         columns = aligned(c * (per * 4 * HDIM), per * 4 * HDIM)
-        return [
-            pltpu.make_async_copy(hbm.at[:, columns], buf.at[:, columns], kv_sem.at[c, which])
-            for which, (hbm, buf) in enumerate(((k_hbm, k_buf), (v_hbm, v_buf)))
-        ]
+        hbm, buf = ((k_hbm, k_buf), (v_hbm, v_buf))[which]
+        return pltpu.make_async_copy(hbm.at[:, columns], buf.at[:, columns], kv_sem.at[c, which])
 
     @pl.loop(0, count)
     def _(c):
-        for copy in loads(c):
-            copy.start()
+        load(c, 0).start()
+        load(c, 1).start()
 
     barrier = pltpu.get_barrier_semaphore()
     for peer in [sibling, across] + [device_at(z_peer(s)) for s in offsets]:
@@ -98,7 +96,7 @@
 
     pl.semaphore_wait(barrier, nz - 1 + 2)
 
-    early = min(2, count - 1) * per
+    early = min(3, count - 1) * per
     sib_base = (1 - core) * (2 * nz)
 
     def piece(i, first, slots=1):
@@ -174,37 +172,38 @@
     def pair_columns(c, pair):
         return aligned((c * pairs + pair) * 2 * HDIM, 2 * HDIM)
 
-    def compute(c, middle):
+    def score(c, pair):
+        quad = c * per + pair // 2
+        q_quad = q_all[:, :, aligned(quad * HDIM, HDIM)].astype(jnp.float32)
+        half = pair % 2
+        q_pair = q_quad[:, 8 * half : 8 * half + 8, :].reshape(rows, HDIM)
+        spread = jnp.concatenate(
+            [jnp.where(first, q_pair, 0.0), jnp.where(first, 0.0, q_pair)], axis=1
+        ).astype(jnp.bfloat16)
+        score_buf[pair] = lax.dot_general(
+            spread, k_buf[:, pair_columns(c, pair)], (((1,), (1,)), ((), ())),
+            preferred_element_type=jnp.float32,
+        )
+
+    def compute(c, following, middle):
         out = part.at[c]
         stats = jnp.zeros((rows, HDIM), jnp.float32)
-        scores = []
+        peaks, totals, split = [], [], []
         for pair in range(pairs):
-            quad = c * per + pair // 2
-            q_quad = q_all[:, :, aligned(quad * HDIM, HDIM)].astype(jnp.float32)
-            half = pair % 2
-            q_pair = q_quad[:, 8 * half : 8 * half + 8, :].reshape(rows, HDIM)
-            spread = jnp.concatenate(
-                [jnp.where(first, q_pair, 0.0), jnp.where(first, 0.0, q_pair)], axis=1
-            ).astype(jnp.bfloat16)
-            scores.append(
-                lax.dot_general(
-                    spread, k_buf[:, pair_columns(c, pair)], (((1,), (1,)), ((), ())),
-                    preferred_element_type=jnp.float32,
-                )
-            )
-        middle(c)
-        peaks = [jnp.max(score, axis=1, keepdims=True) * log_scale for score in scores]
-        weights = [jnp.exp2(score * log_scale - peak) for score, peak in zip(scores, peaks)]
-        split = []
-        for weight in weights:
+            peak = jnp.max(score_buf[pair], axis=1, keepdims=True) * log_scale
+            weight = jnp.exp2(score_buf[pair] * log_scale - peak)
             high = weight.astype(jnp.bfloat16)
             low = (weight - high.astype(jnp.float32)).astype(jnp.bfloat16)
             split.append(jnp.concatenate([high, low], axis=0))
+            peaks.append(peak)
+            totals.append(jnp.sum(weight, axis=1, keepdims=True))
+            if following:
+                score(c + 1, pair)
+        middle(c)
         products = [
             jnp.dot(split[pair], v_buf[:, pair_columns(c, pair)], preferred_element_type=jnp.float32)
             for pair in range(pairs)
         ]
-        totals = [jnp.sum(weight, axis=1, keepdims=True) for weight in weights]
         for pair in range(pairs):
             summed = products[pair][:rows] + products[pair][rows:]
             picked = jnp.where(first, summed[:, :HDIM], summed[:, HDIM:])
@@ -276,16 +275,25 @@
             late_y_arrival().wait_recv()
             late_core().start()
 
-    @pl.loop(0, count)
+    load(0, 0).wait()
+    for pair in range(pairs):
+        score(0, pair)
+
+    @pl.loop(0, count - 1)
     def _(c):
         @pl.when(c == 2)
         def _():
             late_core_arrival().wait_recv()
 
-        for copy in loads(c):
-            copy.wait()
-        compute(c, advance)
+        load(c + 1, 0).wait()
+        load(c, 1).wait()
+        compute(c, True, advance)
         core_copy(c).start()
+
+    last = count - 1
+    load(last, 1).wait()
+    compute(last, False, advance)
+    core_copy(last).start()
 
     start_z(count - 3)
     start_y(count - 1)
@@ -338,6 +346,7 @@
         pltpu.VMEM((16, quads * HDIM), jnp.float32),
         pltpu.VMEM((n, 16, quads * HDIM), jnp.bfloat16),
         pltpu.VMEM((count, 8, 2 * per * HDIM), jnp.float32),
+        pltpu.VMEM((2 * per, n * 8, tokens), jnp.float32),
     ]
     scratch += [dma((count, 2))] + [dma((2, nz))] * 2 + [dma((nz + 1,))] * 2 + [dma((3,))] * 2
     scratch += [dma((count,))] * 4 + [dma((count, nz))] * 2

time: 36.9 us -> 38.1 us (1.033)
  Pallas kernels: 35.2 us -> 36.5 us
    pallas_call x1, Pallas kernels: 35.2 us -> 36.5 us  [shards(): pl.pallas_call(functools.partial(kernel, n, per), out_shape=jax.ShapeDtyp...]
where the time goes in v8:
time: 38.1 us; the launch traced here: 37.9 us
  Pallas kernels  36.5 us (96%)
  local copies, waits for them, and re-layouts  1.41 us (4%)
    pallas_call x1, Pallas kernels, shards(): pl.pallas_call(functools.partial(kernel, n, per), out_shape=jax.ShapeDtyp...  36.5 us
    unnamed x1, local copies, waits for them, and re-layouts  1.41 us

profile of v8, /device:TPU:0, one launch (start us, length us, event | category | flops | bytes accessed | tf_op | source)
XLA Modules:
  0.0 37.9 jit_solution(10348049838893082304)
XLA Ops:
  0.0 36.5 %shard_map.46 = bf16[4,5120]{1,0:T(4,128)(2,1)} custom-call(bf16[4,5120]{1,0:T(4,128)(2,1)} %q_ref.1, bf16[512,5120]{1,0:T(8,128)(2,1)} %k_hbm.1, bf16[512,5120]{1,0:T(8,128)(2,1)} %v_hbm.1, f32[1,5120]{1,0:T(1,128)} %bitcast.1), custom_call_target="tpu_custom_call" | custom-call | tf_op jit(solution)/shard_map/pallas_call | solution.py:355
  36.5 1.4 %copy.6 = bf16[4,5120]{1,0:T(4,128)(2,1)} copy(bf16[4,5120]{1,0:T(4,128)(2,1)} %shard_map.46) | data formatting | bytes 81920

commit v9 on v2

--- a/solution.py
+++ b/solution.py
@@ -155,39 +155,42 @@
         width = sizes[i] * 2 * HDIM
         out = part[i]
 
-        def quad_step(step, stats):
-            quad = starts[i] + step
+        stats = jnp.zeros((rows, HDIM), jnp.float32)
+        pairs = sizes[i] * 2
+        columns = [pl.ds((starts[i] * 2 + pair) * 2 * HDIM, 2 * HDIM) for pair in range(pairs)]
+        scores = []
+        for pair in range(pairs):
+            quad = starts[i] + pair // 2
             q_quad = q_all[:, :, pl.ds(quad * HDIM, HDIM)].astype(jnp.float32)
-            for half in range(2):
-                q_pair = q_quad[:, 8 * half : 8 * half + 8, :].reshape(rows, HDIM)
-                spread = jnp.concatenate(
-                    [jnp.where(first, q_pair, 0.0), jnp.where(first, 0.0, q_pair)], axis=1
-                ).astype(jnp.bfloat16)
-                at = pl.ds((quad * 2 + half) * 2 * HDIM, 2 * HDIM)
-                scores = lax.dot_general(
-                    spread, k_buf[:, at], (((1,), (1,)), ((), ())),
+            half = pair % 2
+            q_pair = q_quad[:, 8 * half : 8 * half + 8, :].reshape(rows, HDIM)
+            spread = jnp.concatenate(
+                [jnp.where(first, q_pair, 0.0), jnp.where(first, 0.0, q_pair)], axis=1
+            ).astype(jnp.bfloat16)
+            scores.append(
+                lax.dot_general(
+                    spread, k_buf[:, columns[pair]], (((1,), (1,)), ((), ())),
                     preferred_element_type=jnp.float32,
                 )
-                peak = jnp.max(scores, axis=1, keepdims=True) * log_scale
-                weights = jnp.exp2(scores * log_scale - peak)
-                total = jnp.sum(weights, axis=1, keepdims=True)
-                high = weights.astype(jnp.bfloat16)
-                low = (weights - high.astype(jnp.float32)).astype(jnp.bfloat16)
-                both = jnp.dot(
-                    jnp.concatenate([high, low], axis=0), v_buf[:, at],
-                    preferred_element_type=jnp.float32,
-                )
-                summed = both[:rows] + both[rows:]
-                picked = jnp.where(first, summed[:, :HDIM], summed[:, HDIM:])
-                pair = step * 2 + half
-                out[:, :, pl.ds(pair * HDIM, HDIM)] = picked.reshape(n, 8, HDIM)
-                stats = jnp.where(column == pair, peak, stats)
-                stats = jnp.where(column == pair + 64, total, stats)
-            return stats
-
-        stats = jnp.zeros((rows, HDIM), jnp.float32)
-        for step in range(sizes[i]):
-            stats = quad_step(step, stats)
+            )
+        peaks = [jnp.max(score, axis=1, keepdims=True) * log_scale for score in scores]
+        weights = [jnp.exp2(score * log_scale - peak) for score, peak in zip(scores, peaks)]
+        split = []
+        for weight in weights:
+            high = weight.astype(jnp.bfloat16)
+            low = (weight - high.astype(jnp.float32)).astype(jnp.bfloat16)
+            split.append(jnp.concatenate([high, low], axis=0))
+        products = [
+            jnp.dot(split[pair], v_buf[:, columns[pair]], preferred_element_type=jnp.float32)
+            for pair in range(pairs)
+        ]
+        totals = [jnp.sum(weight, axis=1, keepdims=True) for weight in weights]
+        for pair in range(pairs):
+            summed = products[pair][:rows] + products[pair][rows:]
+            picked = jnp.where(first, summed[:, :HDIM], summed[:, HDIM:])
+            out[:, :, pl.ds(pair * HDIM, HDIM)] = picked.reshape(n, 8, HDIM)
+            stats = jnp.where(column == pair, peaks[pair], stats)
+            stats = jnp.where(column == pair + 64, totals[pair], stats)
         out[:, :, width:] = stats.reshape(n, 8, HDIM)
 
     def start_core(i):

time: 37.3 us -> 36.9 us (0.989)
  Pallas kernels: 35.7 us -> 35.3 us
    pallas_call x1, Pallas kernels: 35.7 us -> 35.3 us  [shards(): pl.pallas_call(functools.partial(kernel, n, sizes), out_shape=jax.ShapeDt...]
where the time goes in v9:
time: 36.9 us; the launch traced here: 36.7 us
  Pallas kernels  35.3 us (96%)
  local copies, waits for them, and re-layouts  1.41 us (4%)
    pallas_call x1, Pallas kernels, shards(): pl.pallas_call(functools.partial(kernel, n, sizes), out_shape=jax.ShapeDt...  35.3 us
    unnamed x1, local copies, waits for them, and re-layouts  1.41 us

profile of v9, /device:TPU:0, one launch (start us, length us, event | category | flops | bytes accessed | tf_op | source)
XLA Modules:
  0.0 36.7 jit_solution(4500539589711633918)
XLA Ops:
  0.0 35.3 %shard_map.46 = bf16[4,5120]{1,0:T(4,128)(2,1)} custom-call(bf16[4,5120]{1,0:T(4,128)(2,1)} %q_ref.1, bf16[512,5120]{1,0:T(8,128)(2,1)} %k_hbm.1, bf16[512,5120]{1,0:T(8,128)(2,1)} %v_hbm.1, f32[1,5120]{1,0:T(1,128)} %bitcast.1), custom_call_target="tpu_custom_call" | custom-call | tf_op jit(solution)/shard_map/pallas_call | solution.py:308
  35.3 1.4 %copy.6 = bf16[4,5120]{1,0:T(4,128)(2,1)} copy(bf16[4,5120]{1,0:T(4,128)(2,1)} %shard_map.46) | data formatting | bytes 81920
